TPU v7x, 32 devices: a whole 2x2x4 slice. The times are simulated.
32 devices in a mesh: grp: 2 (over y), smp: 8 (over z, x), par: 2 (over core).
Axes of the slice: x: 2, y: 2, z: 4, core: 2. Of those that a mesh axis runs over, the one named last changes fastest.
Arguments:
- log_derivs: bfloat16 [1536, 2048], P(('grp', 'smp'), 'par'), parts along dimension 0, may hold values from -1 to 1, as said below
- coeffs: float32 [1536], P(('grp', 'smp')), parts along dimension 0, may hold values from -6 to 6
Outputs:
- gram_band: float32 [1536, 480], P(('grp', 'smp'), 'par'), parts along dimension 0
- update: float32 [4096], P(('grp', 'par')), parts along dimension 0
There are 2 independent parts, one for each index of `grp`. A program takes and returns all parts, laid end to end along the dimension named above; each array names one. Nothing has to cross between parts.
Inputs may be any that keep to these rules, and one draw needn't show every extreme that they name: `log_derivs`: entries of order a tenth.
All inputs are finite; a program needn't handle non-finite values.
Results may differ from a plain program's by a relative error of at most 0.0029.
Values may be sent and summed in bfloat16 or wider, within the bound.
A program may use at most 64 MiB of HBM per device.

v0:
```python
import jax
import jax.numpy as jnp
from jax import lax
from jax.sharding import PartitionSpec as P


def from_behind(value, axis, steps):
    count = lax.axis_size(axis)
    pairs = [(source, (source + steps) % count) for source in range(count)]
    return lax.ppermute(value, axis, pairs)


def tile_of(centred, other):
    return lax.dot_general(
        centred, other, (((1,), (1,)), ((), ())), preferred_element_type=jnp.float32
    )


def on_device(log_derivs, coeffs):
    rows = log_derivs.shape[0]
    count = lax.axis_size("smp")
    half = count // 2
    total = lax.psum(jnp.sum(log_derivs.astype(jnp.float32), axis=0), "smp")
    mean = total / (rows * count)
    centred = (log_derivs.astype(jnp.float32) - mean).astype(jnp.bfloat16)
    local_update = jnp.dot(coeffs, centred.astype(jnp.float32), precision=lax.Precision.HIGHEST)
    update = lax.psum(local_update, "smp")
    band_init = jnp.zeros((rows, (half + 1) * rows), jnp.float32)

    def advance(step, carry):
        visitor, band = carry
        band = lax.dynamic_update_slice(band, tile_of(centred, visitor), (0, step * rows))
        visitor = from_behind(visitor, "smp", -1)
        return (visitor, band)

    visitor, band = lax.fori_loop(0, half, advance, (centred, band_init))
    band = lax.dynamic_update_slice(band, tile_of(centred, visitor), (0, half * rows))
    gram_band = lax.psum_scatter(band, "par", scatter_dimension=1, tiled=True)
    return (gram_band, update)


def solution(mesh):
    return jax.shard_map(
        on_device,
        mesh=mesh,
        in_specs=(P(("grp", "smp"), "par"), P(("grp", "smp"))),
        out_specs=(P(("grp", "smp"), "par"), P(("grp", "par"))),
        check_vma=False,
    )
```

profile of v0, /device:TPU:0, one launch (start us, length us, event | category | flops | bytes accessed | tf_op | source)
XLA Modules:
  0.0 95.2 jit_solution(1871745500836312607)
XLA Ops:
  7.2 1.0 %convert_reduce_fusion = f32[1024]{0:T(1024)S(1)} fusion(bf16[96,1024]{1,0:T(8,128)(2,1)} %param.4), kind=kLoop, calls=%fused_computation.2 | loop fusion | flops 195584 | bytes 200704 | tf_op jit(solution)/shard_map/reduce_sum | solution.py:23
  8.2 23.2 %psum.14 = f32[1024]{0:T(1024)S(1)} all-reduce(f32[1024]{0:T(1024)S(1)} %convert_reduce_fusion), channel_id=1, replica_groups=mesh['grp'=2,'smp'=8,'par'=2] {'smp'}, use_global_device_ids=true, to_apply=%region_1.0 | all-reduce | flops 1024 | bytes 8192 | tf_op jit(solution)/shard_map/psum | solution.py:23
  31.6 31.0 %while.15 = (s32[]{:T(128)}, bf16[96,1024]{1,0:T(8,128)(2,1)S(1)}, f32[96,480]{1,0:T(8,128)S(1)}, bf16[96,1024]{1,0:T(8,128)(2,1)S(1)}, s32[]{:T(128)}, /*index=5*/s32[]{:T(128)}, s32[]{:T(128)}, s32[]{:T(128)}) while((s32[]{:T(128)}, bf16[96,1024]{1,0:T(8,128)(2,1)S(1)}, f32[96,480]{1,0:T(8,128)S(1)}, bf16[96,1024]{1,0:T(8,128)(2,1)S(1)}, ...), condition=%wide.region_3.0_spmd, body=%wide.region_2.0_spmd.sunk | while | flops 18874368 | bytes 1683631 | solution.py:36
  31.6 0.1 collective-permute-start
  31.7 0.2 fusion.14
  31.9 0.6 dynamic_update_slice.13
  32.4 6.6 %collective-permute-done = bf16[96,1024]{1,0:T(8,128)(2,1)S(1)} collective-permute-done((bf16[96,1024]{1,0:T(8,128)(2,1)S(1)}, bf16[96,1024]{1,0:T(8,128)(2,1)S(1)}, u32[]{:S(2)}, u32[]{:S(2)}) %collective-permute-start) | collective-permute-done | bytes 196640 | tf_op jit(solution)/shard_map/while/body/eval_jaxpr/ppermute | solution.py:10
  39.1 1.0 %collective-permute-start = (bf16[96,1024]{1,0:T(8,128)(2,1)S(1)}, bf16[96,1024]{1,0:T(8,128)(2,1)S(1)}, u32[]{:S(2)}, u32[]{:S(2)}) collective-permute-start(bf16[96,1024]{1,0:T(8,128)(2,1)S(1)} %copy.11), channel_id=1, source_target_pairs={{0,14},{2,0},{4,2},{6,4},{8,6},{10,8},{12,10},{14,12},{1,15},{3,1}... | collective-permute-start | bytes 589832 | tf_op jit(solution)/shard_map/while/body/eval_jaxpr/ppermute | solution.py:10
  40.1 0.2 fusion.14
  40.3 0.7 dynamic_update_slice.13
  41.0 4.8 %collective-permute-done = bf16[96,1024]{1,0:T(8,128)(2,1)S(1)} collective-permute-done((bf16[96,1024]{1,0:T(8,128)(2,1)S(1)}, bf16[96,1024]{1,0:T(8,128)(2,1)S(1)}, u32[]{:S(2)}, u32[]{:S(2)}) %collective-permute-start) | collective-permute-done | bytes 196640 | tf_op jit(solution)/shard_map/while/body/eval_jaxpr/ppermute | solution.py:10
  45.8 3.3 %collective-permute-start = (bf16[96,1024]{1,0:T(8,128)(2,1)S(1)}, bf16[96,1024]{1,0:T(8,128)(2,1)S(1)}, u32[]{:S(2)}, u32[]{:S(2)}) collective-permute-start(bf16[96,1024]{1,0:T(8,128)(2,1)S(1)} %copy.11), channel_id=1, source_target_pairs={{0,14},{2,0},{4,2},{6,4},{8,6},{10,8},{12,10},{14,12},{1,15},{3,1}... | collective-permute-start | bytes 589832 | tf_op jit(solution)/shard_map/while/body/eval_jaxpr/ppermute | solution.py:10
  49.1 0.2 fusion.14
  49.4 0.7 dynamic_update_slice.13
  50.1 4.0 %collective-permute-done = bf16[96,1024]{1,0:T(8,128)(2,1)S(1)} collective-permute-done((bf16[96,1024]{1,0:T(8,128)(2,1)S(1)}, bf16[96,1024]{1,0:T(8,128)(2,1)S(1)}, u32[]{:S(2)}, u32[]{:S(2)}) %collective-permute-start) | collective-permute-done | bytes 196640 | tf_op jit(solution)/shard_map/while/body/eval_jaxpr/ppermute | solution.py:10
  54.1 5.2 %collective-permute-start = (bf16[96,1024]{1,0:T(8,128)(2,1)S(1)}, bf16[96,1024]{1,0:T(8,128)(2,1)S(1)}, u32[]{:S(2)}, u32[]{:S(2)}) collective-permute-start(bf16[96,1024]{1,0:T(8,128)(2,1)S(1)} %copy.11), channel_id=1, source_target_pairs={{0,14},{2,0},{4,2},{6,4},{8,6},{10,8},{12,10},{14,12},{1,15},{3,1}... | collective-permute-start | bytes 589832 | tf_op jit(solution)/shard_map/while/body/eval_jaxpr/ppermute | solution.py:10
  59.4 0.2 fusion.14
  59.6 0.7 dynamic_update_slice.13
  60.3 2.3 %collective-permute-done = bf16[96,1024]{1,0:T(8,128)(2,1)S(1)} collective-permute-done((bf16[96,1024]{1,0:T(8,128)(2,1)S(1)}, bf16[96,1024]{1,0:T(8,128)(2,1)S(1)}, u32[]{:S(2)}, u32[]{:S(2)}) %collective-permute-start) | collective-permute-done | bytes 196640 | tf_op jit(solution)/shard_map/while/body/eval_jaxpr/ppermute | solution.py:10
  62.6 0.2 convolution_dynamic-update-slice_fusion
  62.8 0.8 copy.4
  63.7 0.2 fusion.1
  63.8 22.9 %psum.15 = f32[1024]{0:T(1024)} all-reduce(f32[1024]{0:T(1024)S(1)} %bitcast.17), channel_id=1, replica_groups=mesh['grp'=2,'smp'=8,'par'=2] {'smp'}, use_global_device_ids=true, to_apply=%region_5.0 | all-reduce | flops 1024 | bytes 8192 | tf_op jit(solution)/shard_map/psum | solution.py:27
  86.8 1.6 %copy.5 = f32[96,240]{1,0:T(8,128)} copy(f32[96,240]{0,1:T(8,128)} %bitcast.16) | data formatting | bytes 184320
  (15 shorter events, 0.2 us)
Async XLA Ops:
  7.2 56.5 %copy-start = (f32[96]{0:T(128)S(1)}, f32[96]{0:T(128)}, u32[]{:S(2)}) copy-start(f32[96]{0:T(128)} %param.5) | copy-start | bytes 1156
  7.2 24.3 %copy-start.1 = (bf16[96,1024]{1,0:T(8,128)(2,1)S(1)}, bf16[96,1024]{1,0:T(8,128)(2,1)}, u32[]{:S(2)}) copy-start(bf16[96,1024]{1,0:T(8,128)(2,1)} %param.4) | copy-start | bytes 589828
  7.2 79.6 %reduce-scatter.4.cloned.1.call-start = ((), (), s32[]{:S(2)}) async-start(), calls=%async_computation.1 | async-start | bytes 368640
  31.6 7.5 %collective-permute-start = (bf16[96,1024]{1,0:T(8,128)(2,1)S(1)}, bf16[96,1024]{1,0:T(8,128)(2,1)S(1)}, u32[]{:S(2)}, u32[]{:S(2)}) collective-permute-start(bf16[96,1024]{1,0:T(8,128)(2,1)S(1)} %copy.11), channel_id=1, source_target_pairs={{0,14},{2,0},{4,2},{6,4},{8,6},{10,8},{12,10},{14,12},{1,15},{3,1}... | collective-permute-start | bytes 589832 | tf_op jit(solution)/shard_map/while/body/eval_jaxpr/ppermute | solution.py:10
  39.1 6.7 %collective-permute-start = (bf16[96,1024]{1,0:T(8,128)(2,1)S(1)}, bf16[96,1024]{1,0:T(8,128)(2,1)S(1)}, u32[]{:S(2)}, u32[]{:S(2)}) collective-permute-start(bf16[96,1024]{1,0:T(8,128)(2,1)S(1)} %copy.11), channel_id=1, source_target_pairs={{0,14},{2,0},{4,2},{6,4},{8,6},{10,8},{12,10},{14,12},{1,15},{3,1}... | collective-permute-start | bytes 589832 | tf_op jit(solution)/shard_map/while/body/eval_jaxpr/ppermute | solution.py:10
  45.8 8.3 %collective-permute-start = (bf16[96,1024]{1,0:T(8,128)(2,1)S(1)}, bf16[96,1024]{1,0:T(8,128)(2,1)S(1)}, u32[]{:S(2)}, u32[]{:S(2)}) collective-permute-start(bf16[96,1024]{1,0:T(8,128)(2,1)S(1)} %copy.11), channel_id=1, source_target_pairs={{0,14},{2,0},{4,2},{6,4},{8,6},{10,8},{12,10},{14,12},{1,15},{3,1}... | collective-permute-start | bytes 589832 | tf_op jit(solution)/shard_map/while/body/eval_jaxpr/ppermute | solution.py:10
  54.1 8.5 %collective-permute-start = (bf16[96,1024]{1,0:T(8,128)(2,1)S(1)}, bf16[96,1024]{1,0:T(8,128)(2,1)S(1)}, u32[]{:S(2)}, u32[]{:S(2)}) collective-permute-start(bf16[96,1024]{1,0:T(8,128)(2,1)S(1)} %copy.11), channel_id=1, source_target_pairs={{0,14},{2,0},{4,2},{6,4},{8,6},{10,8},{12,10},{14,12},{1,15},{3,1}... | collective-permute-start | bytes 589832 | tf_op jit(solution)/shard_map/while/body/eval_jaxpr/ppermute | solution.py:10
Sparse Core Ops, SparseCore 0:
  63.8 9.5 reduce-scatter.3
where the time goes:
time: 95.4 us; the launch traced here: 95.2 us
  blocking collectives  46.1 us (48%)
  waiting for transfers between devices  17.7 us (19%)
  between operations  14.1 us (15%)
  starting transfers between devices  9.68 us (10%)
  local copies, waits for them, and re-layouts  5.3 us (6%)
  matrix products  1.18 us (1%)
  other arithmetic  1.06 us (1%)
    psum x1, blocking collectives, on_device(): total = lax.psum(jnp.sum(log_derivs.astype(jnp.float32), axis=0), 'smp')  23.2 us
    psum x1, blocking collectives, on_device(): update = lax.psum(local_update, 'smp')  22.9 us
    ppermute x4, waiting for transfers between devices, from_behind(): return lax.ppermute(value, axis, pairs)  17.7 us
    ppermute x4, starting transfers between devices, from_behind(): return lax.ppermute(value, axis, pairs)  9.64 us
    dynamic_update_slice x4, local copies, waits for them, and re-layouts, advance(): lax.dynamic_update_slice(band, tile_of(centred, visitor), (0, step * rows))  2.76 us
    unnamed x7, local copies, waits for them, and re-layouts  2.48 us
  transfers between devices with their start and end apart: 5, of which 4 were waited for; matrix products, arithmetic and copies ran while one was open for 4% of the time, Pallas kernels for 0%

commit v1 on v0

v1 whole, which is shorter than its diff:
```python
import functools

import jax
import jax.numpy as jnp
from jax import lax
from jax.experimental import pallas as pl
from jax.experimental.pallas import tpu as pltpu
from jax.sharding import PartitionSpec as P

CHUNKS = 3
UNROLL = 16


def each(low, high, body):
    if high - low <= UNROLL:
        for step in range(low, high):
            body(step)
    else:
        lax.fori_loop(low, high, lambda step, _: (body(step), 0)[1], 0)


def kernel(
    count, x_hbm, c_ref, gram_ref, update_ref,
    slots, cent, stats, part, got,
    load_sem, stat_send, stat_recv, block_send, block_recv, swap_send, swap_recv,
):
    half = count // 2
    depth = half // 2
    rows, cols = slots.shape[1], slots.shape[2]
    width = part.shape[1]
    piece = rows // CHUNKS
    me = lax.axis_index("smp")
    core = lax.axis_index("par")
    bit = lax.rem(me, 2)

    def at(steps):
        return lax.rem(me + steps + count, count)

    load = pltpu.make_async_copy(x_hbm, slots.at[0], load_sem)
    load.start()
    barrier = pltpu.get_barrier_semaphore()
    each(1, count, lambda j: pl.semaphore_signal(barrier, inc=1, device_id={"smp": at(j)}))
    pl.semaphore_signal(barrier, inc=1, device_id={"par": 1 - core})

    c = c_ref[...]
    c1 = c.astype(jnp.bfloat16).astype(jnp.float32)
    c2 = (c - c1).astype(jnp.bfloat16).astype(jnp.float32)
    c3 = c - c1 - c2
    row = lax.broadcasted_iota(jnp.int32, (16, rows), 0)
    weights = jnp.where(row == 0, 1.0, jnp.where(row == 1, c1, jnp.where(row == 2, c2, jnp.where(row == 3, c3, 0.0))))
    load.wait()
    sums = jnp.dot(weights.astype(jnp.bfloat16), slots[0], preferred_element_type=jnp.float32)
    stats[me, 0:1, :] = sums[0:1]
    stats[me, 1:2, :] = sums[1:2] + sums[2:3] + sums[3:4]
    stats[me, 2:3, :] = jnp.broadcast_to(jnp.sum(c, axis=1, keepdims=True), (1, cols))
    stats[me, 3:4, :] = jnp.zeros((1, cols), jnp.float32)
    pl.semaphore_wait(barrier, count)

    def stat_copy(steps):
        return pltpu.make_async_remote_copy(
            src_ref=stats.at[me], dst_ref=stats.at[me],
            send_sem=stat_send.at[steps], recv_sem=stat_recv.at[me],
            device_id={"smp": at(steps)},
        )

    def stat_arrival(steps):
        other = at(steps)
        return pltpu.make_async_remote_copy(
            src_ref=stats.at[other], dst_ref=stats.at[other],
            send_sem=stat_send.at[steps], recv_sem=stat_recv.at[other],
            device_id={"smp": other},
        )

    def block_copy(source, target, chunk, steps):
        span = pl.ds(chunk * piece, piece)
        return pltpu.make_async_remote_copy(
            src_ref=slots.at[source, span], dst_ref=slots.at[target, span],
            send_sem=block_send.at[target, chunk], recv_sem=block_recv.at[target, chunk],
            device_id={"smp": at(steps)},
        )

    mate = 1 - 2 * bit
    each(1, count, lambda j: stat_copy(j).start())

    def send_column(d):
        for chunk in range(CHUNKS):
            block_copy(0, 2 * d, chunk, -2 * d).start()

    @pl.when(bit == 1)
    def _():
        for chunk in range(CHUNKS):
            block_copy(0, 1, chunk, -1).start()

    each(1, depth + 1, send_column)

    each(1, count, lambda j: stat_arrival(j).wait_recv())
    total = jnp.sum(stats[...], axis=0)
    mean = total[0:1] / (rows * count)
    update_ref[...] = total[1:2] - mean * total[2:3]

    def centre(k):
        value = (slots[k].astype(jnp.float32) - mean).astype(jnp.bfloat16)
        cent[pl.ds(pl.multiple_of(k * rows, 16), rows), :] = value

    centre(0)

    def column_arrival(d):
        for chunk in range(CHUNKS):
            block_copy(0, 2 * d, chunk, -2 * d).wait_recv()

            @pl.when(bit == 0)
            def _():
                block_copy(2 * d, 2 * d - 1, chunk, 1).start()

            @pl.when(jnp.logical_and(bit == 1, d < depth))
            def _():
                block_copy(2 * d, 2 * d + 1, chunk, -1).start()

        centre(2 * d)

    each(1, depth + 1, column_arrival)

    def row_arrival(e):
        for chunk in range(CHUNKS):
            block_copy(0, 2 * e - 1, chunk, mate).wait_recv()
        centre(2 * e - 1)

    each(1, depth + 1, row_arrival)

    def tiles(which):
        other = cent[pl.ds(pl.multiple_of(which * width, 16), width), :]
        return lax.dot_general(
            cent[0:rows, :], other, (((1,), (1,)), ((), ())), preferred_element_type=jnp.float32
        )

    part[...] = tiles(1 - core)
    swap = pltpu.make_async_remote_copy(
        src_ref=part, dst_ref=got, send_sem=swap_send, recv_sem=swap_recv, device_id={"par": 1 - core},
    )
    swap.start()
    mine = tiles(core)

    each(1, count, lambda j: stat_copy(j).wait_send())

    def finish(k):
        for chunk in range(CHUNKS):
            block_copy(0, k, chunk, -2).wait_send()

    each(1, half + 1, finish)
    swap.wait()
    gram_ref[...] = mine + got[...]


def on_device(log_derivs, coeffs):
    rows, cols = log_derivs.shape
    count = lax.axis_size("smp")
    half = count // 2
    width = (half + 1) * rows // lax.axis_size("par")
    block = rows * cols * 2
    gram, update = pl.pallas_call(
        functools.partial(kernel, count),
        out_shape=(
            jax.ShapeDtypeStruct((rows, width), jnp.float32),
            jax.ShapeDtypeStruct((1, cols), jnp.float32),
        ),
        in_specs=[pl.BlockSpec(memory_space=pl.ANY), pl.BlockSpec(memory_space=pltpu.VMEM)],
        out_specs=(pl.BlockSpec(memory_space=pltpu.VMEM), pl.BlockSpec(memory_space=pltpu.VMEM)),
        scratch_shapes=[
            pltpu.VMEM((half + 1, rows, cols), jnp.bfloat16),
            pltpu.VMEM(((half + 1) * rows, cols), jnp.bfloat16),
            pltpu.VMEM((count, 4, cols), jnp.float32),
            pltpu.VMEM((rows, width), jnp.float32),
            pltpu.VMEM((rows, width), jnp.float32),
            pltpu.SemaphoreType.DMA,
            pltpu.SemaphoreType.DMA((count,)),
            pltpu.SemaphoreType.DMA((count,)),
            pltpu.SemaphoreType.DMA((half + 1, CHUNKS)),
            pltpu.SemaphoreType.DMA((half + 1, CHUNKS)),
            pltpu.SemaphoreType.DMA,
            pltpu.SemaphoreType.DMA,
        ],
        compiler_params=pltpu.CompilerParams(
            collective_id=0,
            has_side_effects=True,
            vmem_limit_bytes=min(56, 12 + (half + 1)) * 2**20 if half > 16 else 16 * 2**20,
        ),
        cost_estimate=pl.CostEstimate(
            flops=4 * rows * cols * width, bytes_accessed=2 * block, transcendentals=0
        ),
    )(log_derivs, coeffs.reshape(1, rows))
    return gram, update.reshape(cols)


def solution(mesh):
    return jax.shard_map(
        on_device,
        mesh=mesh,
        in_specs=(P(("grp", "smp"), "par"), P(("grp", "smp"))),
        out_specs=(P(("grp", "smp"), "par"), P(("grp", "par"))),
        check_vma=False,
    )
```

time: 95.4 us -> 30.7 us (0.32)
  the two profiles are of different devices: /device:TPU:0 before, /device:TPU:31 now
where the time goes in v1:
time: 30.7 us; the launch traced here: 30.5 us
  Pallas kernels  27 us (88%)
  local copies, waits for them, and re-layouts  2.81 us (9%)
  between operations  0.65 us (2%)
    pallas_call x1, Pallas kernels, on_device(): pl.pallas_call(functools.partial(kernel, count), out_shape=(jax.ShapeDtyp...  27 us
    unnamed x6, local copies, waits for them, and re-layouts  2.81 us

profile of v1, /device:TPU:31, one launch (start us, length us, event | category | flops | bytes accessed | tf_op | source)
XLA Modules:
  0.0 30.5 jit_solution(2155194468329234581)
XLA Ops:
  0.6 0.0 copy-start.1
  0.6 0.6 %copy-done.1 = f32[96]{0:T(128)S(1)} copy-done((f32[96]{0:T(128)S(1)}, f32[96]{0:T(128)}, u32[]{:S(2)}) %copy-start.1) | copy-done | bytes 408
  1.3 0.0 copy-start
  1.3 0.9 %copy-done = bf16[96,1024]{1,0:T(8,128)(2,1)S(1)} copy-done((bf16[96,1024]{1,0:T(8,128)(2,1)S(1)}, bf16[96,1024]{1,0:T(8,128)(2,1)}, u32[]{:S(2)}) %copy-start) | copy-done | bytes 196632
  2.2 27.0 %shard_map.41 = (f32[96,240]{1,0:T(8,128)S(1)}, f32[1,1024]{1,0:T(1,128)S(1)}) custom-call(bf16[96,1024]{1,0:T(8,128)(2,1)S(1)} %copy-done, f32[1,96]{1,0:T(1,128)S(1)} %bitcast.3), custom_call_target="tpu_custom_call" | custom-call | flops 94371840 | bytes 393216 | tf_op jit(solution)/shard_map/pallas_call | solution.py:160
  29.2 0.6 %copy.6 = f32[96,240]{1,0:T(8,128)} copy(f32[96,240]{1,0:T(8,128)S(1)} %get-tuple-element.8) | data formatting | bytes 184320
  29.9 0.6 %copy.7 = f32[1024]{0:T(1024)} copy(f32[1024]{0:T(1024)S(1)} %bitcast.2) | data formatting | bytes 8192
Async XLA Ops:
  0.6 0.7 %copy-start.1 = (f32[96]{0:T(128)S(1)}, f32[96]{0:T(128)}, u32[]{:S(2)}) copy-start(f32[96]{0:T(128)} %param.3) | copy-start | bytes 1156
  1.3 0.9 %copy-start = (bf16[96,1024]{1,0:T(8,128)(2,1)S(1)}, bf16[96,1024]{1,0:T(8,128)(2,1)}, u32[]{:S(2)}) copy-start(bf16[96,1024]{1,0:T(8,128)(2,1)} %x_hbm.1) | copy-start | bytes 589828

commit v2 on v0

v2 whole, which is shorter than its diff:
```python
import functools

import jax
import jax.numpy as jnp
from jax import lax
from jax.experimental import pallas as pl
from jax.experimental.pallas import tpu as pltpu
from jax.sharding import PartitionSpec as P

CHUNKS = 3
UNROLL = 16


def each(low, high, body):
    if high - low <= UNROLL:
        for step in range(low, high):
            body(step)
    else:
        lax.fori_loop(low, high, lambda step, _: (body(step), 0)[1], 0)


def kernel(
    count, x_hbm, c_hbm, gram_ref, update_ref,
    slots, cent, c_ref, stats, part, got,
    load_sem, c_sem, sum_send, sum_recv, up_send, up_recv,
    down_send, entry_send, cross_send, block_recv, tile_send, tile_recv,
):
    half = count // 2
    depth = half // 2
    lines = count // 2
    middle = half // 2
    rows, cols = slots.shape[1], slots.shape[2]
    lanes = cols // 8
    width = gram_ref.shape[1]
    piece = rows // CHUNKS
    me = lax.axis_index("smp")
    core = lax.axis_index("par")
    line, bit = lax.div(me, 2), lax.rem(me, 2)
    mate = 1 - 2 * bit

    def at(steps):
        return lax.rem(me + steps + count, count)

    load = pltpu.make_async_copy(x_hbm, slots.at[0], load_sem)
    load.start()
    c_load = pltpu.make_async_copy(c_hbm, c_ref, c_sem)
    c_load.start()
    barrier = pltpu.get_barrier_semaphore()
    each(1, count, lambda j: pl.semaphore_signal(barrier, inc=1, device_id={"smp": at(j)}))
    pl.semaphore_signal(barrier, inc=1, device_id={"par": 1 - core})

    def pack(value):
        return jnp.concatenate([value[:, lanes * j : lanes * (j + 1)] for j in range(8)], axis=0)

    def unpack(value):
        return jnp.concatenate([value[j : j + 1, :] for j in range(8)], axis=1)

    load.wait()
    stats[0, me] = pack(jnp.sum(slots[0].astype(jnp.float32), axis=0, keepdims=True))
    c_load.wait()
    pl.semaphore_wait(barrier, count)

    def stat_copy(kind, source, steps):
        send, recv = ((sum_send, sum_recv), (up_send, up_recv))[kind]
        return pltpu.make_async_remote_copy(
            src_ref=stats.at[kind, source], dst_ref=stats.at[kind, source],
            send_sem=send.at[steps], recv_sem=recv.at[source],
            device_id={"smp": at(steps)},
        )

    def block_copy(source, target, chunk, send, device):
        span = pl.ds(pl.multiple_of(chunk * piece, 16), piece)
        return pltpu.make_async_remote_copy(
            src_ref=slots.at[source, span], dst_ref=slots.at[target, span],
            send_sem=send, recv_sem=block_recv.at[target, chunk],
            device_id={"smp": device},
        )

    def down(d, chunk):
        return block_copy(2 * d, 2 * d + 2, chunk, down_send.at[d, chunk], at(-2))

    def up(d, chunk):
        return block_copy(2 * d, 2 * d - 2, chunk, down_send.at[d, chunk], at(2))

    def entry(chunk):
        return block_copy(0, half, chunk, entry_send.at[chunk], at(-2 * depth))

    def cross(d, chunk):
        return block_copy(2 * d, 2 * d - mate, chunk, cross_send.at[d, chunk], at(mate))

    each(1, count, lambda j: stat_copy(0, me, j).start())

    for chunk in range(CHUNKS):
        @pl.when(bit == 1)
        def _():
            cross(0, chunk).start()

        @pl.when(line > 0)
        def _():
            down(0, chunk).start()

        @pl.when(line < depth)
        def _():
            entry(chunk).start()

    each(1, count, lambda j: stat_copy(0, at(j), j).wait_recv())
    mean = unpack(jnp.sum(stats[0], axis=0)) / (rows * count)

    def tile_copy(k, low, size):
        span = pl.ds(pl.multiple_of(low, 16), size)
        return pltpu.make_async_remote_copy(
            src_ref=part.at[span], dst_ref=got.at[span],
            send_sem=tile_send.at[k], recv_sem=tile_recv.at[k],
            device_id={"par": 1 - core},
        )

    def tile_whole(k):
        return tile_copy(k, k * rows, rows)

    def tile_split(side):
        return tile_copy(middle, middle * rows + side * (rows // 2), rows // 2)

    def process(k):
        value = (slots[k].astype(jnp.float32) - mean).astype(jnp.bfloat16)
        if isinstance(k, int) and k == 0:
            cent[...] = value
        span = pl.ds(pl.multiple_of(k * rows, 16), rows)
        part[span, :] = lax.dot_general(
            value, cent[...], (((1,), (1,)), ((), ())), preferred_element_type=jnp.float32
        )

        @pl.when(jnp.logical_or(jnp.logical_and(k > middle, core == 0), jnp.logical_and(k < middle, core == 1)))
        def _():
            tile_whole(k).start()

        @pl.when(k == middle)
        def _():
            tile_split(1 - core).start()

    process(0)

    c = c_ref[...]
    c1 = c.astype(jnp.bfloat16).astype(jnp.float32)
    c2 = (c - c1).astype(jnp.bfloat16).astype(jnp.float32)
    c3 = c - c1 - c2
    row = lax.broadcasted_iota(jnp.int32, (16, rows), 0)
    weights = jnp.where(row == 0, c1, jnp.where(row == 1, c2, jnp.where(row == 2, c3, 0.0)))
    sums = jnp.dot(weights.astype(jnp.bfloat16), cent[...], preferred_element_type=jnp.float32)
    stats[1, me] = pack(sums[0:1] + sums[1:2] + sums[2:3])
    each(1, count, lambda j: stat_copy(1, me, j).start())

    wraps = line + depth >= lines

    def arrival(step):
        d = jnp.where(wraps, depth - lax.rem(step, depth), 1 + lax.div(step, CHUNKS))
        chunk = jnp.where(wraps, lax.div(step, depth), lax.rem(step, CHUNKS))
        block_copy(2 * d, 2 * d, chunk, down_send.at[d, chunk], at(2)).wait_recv()
        inside = line + d < lines

        @pl.when(jnp.logical_or(bit == 0, d < depth))
        def _():
            cross(d, chunk).start()

        @pl.when(jnp.logical_and(inside, jnp.logical_and(d < depth, line > 0)))
        def _():
            down(d, chunk).start()

        @pl.when(jnp.logical_and(jnp.logical_not(inside), jnp.logical_and(d > 1, line < lines - 1)))
        def _():
            up(d, chunk).start()

    each(0, depth * CHUNKS, lambda step: arrival(jnp.int32(step)))

    def pair(e):
        process(2 * e)
        for chunk in range(CHUNKS):
            block_copy(0, 2 * e - 1, chunk, entry_send.at[chunk], at(mate)).wait_recv()
        process(2 * e - 1)

    each(1, depth + 1, pair)

    for chunk in range(CHUNKS):
        @pl.when(line > 0)
        def _():
            down(0, chunk).wait_send()

        @pl.when(line < depth)
        def _():
            entry(chunk).wait_send()

        @pl.when(bit == 1)
        def _():
            cross(0, chunk).wait_send()

    def leave(d):
        inside = line + d < lines
        for chunk in range(CHUNKS):
            @pl.when(jnp.logical_or(bit == 0, d < depth))
            def _():
                cross(d, chunk).wait_send()

            @pl.when(jnp.logical_and(inside, jnp.logical_and(d < depth, line > 0)))
            def _():
                down(d, chunk).wait_send()

            @pl.when(jnp.logical_and(jnp.logical_not(inside), jnp.logical_and(d > 1, line < lines - 1)))
            def _():
                up(d, chunk).wait_send()

    each(1, depth + 1, leave)
    each(1, count, lambda j: stat_copy(0, me, j).wait_send())
    each(1, count, lambda j: stat_copy(1, me, j).wait_send())
    each(1, count, lambda j: stat_copy(1, at(j), j).wait_recv())
    update_ref[...] = unpack(jnp.sum(stats[1], axis=0))

    def swapped(k):
        @pl.when(jnp.logical_or(jnp.logical_and(k > middle, core == 0), jnp.logical_and(k < middle, core == 1)))
        def _():
            tile_whole(k).wait_send()

        @pl.when(jnp.logical_or(jnp.logical_and(k > middle, core == 1), jnp.logical_and(k < middle, core == 0)))
        def _():
            tile_whole(k).wait_recv()

        @pl.when(k == middle)
        def _():
            tile_split(1 - core).wait_send()
            tile_split(core).wait_recv()

    each(0, half + 1, swapped)
    mine = pl.ds(pl.multiple_of(core * width, 16), width)
    gram_ref[...] = (part[mine, :] + got[mine, :]).T


def on_device(log_derivs, coeffs):
    rows, cols = log_derivs.shape
    count = lax.axis_size("smp")
    half = count // 2
    depth = half // 2
    band = (half + 1) * rows
    width = band // lax.axis_size("par")
    block = rows * cols * 2
    dma = pltpu.SemaphoreType.DMA
    gram, update = pl.pallas_call(
        functools.partial(kernel, count),
        out_shape=(
            jax.ShapeDtypeStruct((rows, width), jnp.float32),
            jax.ShapeDtypeStruct((1, cols), jnp.float32),
        ),
        in_specs=[pl.BlockSpec(memory_space=pltpu.HBM)] * 2,
        out_specs=(pl.BlockSpec(memory_space=pltpu.VMEM), pl.BlockSpec(memory_space=pltpu.VMEM)),
        scratch_shapes=[
            pltpu.VMEM((half + 1, rows, cols), jnp.bfloat16),
            pltpu.VMEM((rows, cols), jnp.bfloat16),
            pltpu.VMEM((1, rows), jnp.float32),
            pltpu.VMEM((2, count, 8, cols // 8), jnp.float32),
            pltpu.VMEM((band, rows), jnp.float32),
            pltpu.VMEM((band, rows), jnp.float32),
            dma, dma,
            dma((count,)), dma((count,)), dma((count,)), dma((count,)),
            dma((depth + 1, CHUNKS)), dma((CHUNKS,)), dma((depth + 1, CHUNKS)),
            dma((half + 1, CHUNKS)), dma((half + 1,)), dma((half + 1,)),
        ],
        compiler_params=pltpu.CompilerParams(
            collective_id=0,
            has_side_effects=True,
            vmem_limit_bytes=48 * 2**20 if half > 16 else 16 * 2**20,
        ),
        cost_estimate=pl.CostEstimate(
            flops=4 * rows * cols * width, bytes_accessed=2 * block, transcendentals=0
        ),
    )(log_derivs, coeffs.reshape(1, rows))
    return gram, update.reshape(cols)


def solution(mesh):
    return jax.shard_map(
        on_device,
        mesh=mesh,
        in_specs=(P(("grp", "smp"), "par"), P(("grp", "smp"))),
        out_specs=(P(("grp", "smp"), "par"), P(("grp", "par"))),
        check_vma=False,
    )
```

time: 95.4 us -> 27.7 us (0.29)
  the two profiles are of different devices: /device:TPU:0 before, /device:TPU:31 now
where the time goes in v2:
time: 27.7 us; the launch traced here: 27.6 us
  Pallas kernels  24.1 us (87%)
  local copies, waits for them, and re-layouts  2.81 us (10%)
  between operations  0.65 us (2%)
    pallas_call x1, Pallas kernels, on_device(): pl.pallas_call(functools.partial(kernel, count), out_shape=(jax.ShapeDtyp...  24.1 us
    unnamed x6, local copies, waits for them, and re-layouts  2.81 us

profile of v2, /device:TPU:31, one launch (start us, length us, event | category | flops | bytes accessed | tf_op | source)
XLA Modules:
  0.0 27.6 jit_solution(5243852215683801564)
XLA Ops:
  0.6 0.0 copy-start.1
  0.6 0.6 %copy-done.1 = f32[96]{0:T(128)S(1)} copy-done((f32[96]{0:T(128)S(1)}, f32[96]{0:T(128)}, u32[]{:S(2)}) %copy-start.1) | copy-done | bytes 408
  1.3 0.0 copy-start
  1.3 0.9 %copy-done = bf16[96,1024]{1,0:T(8,128)(2,1)S(1)} copy-done((bf16[96,1024]{1,0:T(8,128)(2,1)S(1)}, bf16[96,1024]{1,0:T(8,128)(2,1)}, u32[]{:S(2)}) %copy-start) | copy-done | bytes 196632
  2.2 24.1 %shard_map.41 = (f32[96,240]{1,0:T(8,128)S(1)}, f32[1,1024]{1,0:T(1,128)S(1)}) custom-call(bf16[96,1024]{1,0:T(8,128)(2,1)S(1)} %copy-done, f32[1,96]{1,0:T(1,128)S(1)} %bitcast.3), custom_call_target="tpu_custom_call" | custom-call | flops 94371840 | bytes 393216 | tf_op jit(solution)/shard_map/pallas_call | solution.py:244
  26.4 0.6 %copy.6 = f32[96,240]{1,0:T(8,128)} copy(f32[96,240]{1,0:T(8,128)S(1)} %get-tuple-element.8) | data formatting | bytes 184320
  27.0 0.6 %copy.7 = f32[1024]{0:T(1024)} copy(f32[1024]{0:T(1024)S(1)} %bitcast.2) | data formatting | bytes 8192
Async XLA Ops:
  0.6 0.7 %copy-start.1 = (f32[96]{0:T(128)S(1)}, f32[96]{0:T(128)}, u32[]{:S(2)}) copy-start(f32[96]{0:T(128)} %param.3) | copy-start | bytes 1156
  1.3 0.9 %copy-start = (bf16[96,1024]{1,0:T(8,128)(2,1)S(1)}, bf16[96,1024]{1,0:T(8,128)(2,1)}, u32[]{:S(2)}) copy-start(bf16[96,1024]{1,0:T(8,128)(2,1)} %x_hbm.1) | copy-start | bytes 589828

commit v3 on v2

v3 whole, which is shorter than its diff:
```python
import functools

import jax
import jax.numpy as jnp
from jax import lax
from jax.experimental import pallas as pl
from jax.experimental.pallas import tpu as pltpu
from jax.sharding import PartitionSpec as P

CHUNKS = 6
FIRST = 2
MEAN_AFTER = 4
UNROLL = 16


def each(low, high, body):
    if high - low <= UNROLL:
        for step in range(low, high):
            body(step)
    else:
        lax.fori_loop(low, high, lambda step, _: (body(step), 0)[1], 0)


def kernel(
    count, x_hbm, c_hbm, gram_ref, update_ref,
    slots, cent, c_ref, pairs, stats, parts, band, spare,
    load_sem, c_sem, above, below, pair_send, pair_recv, stat_send, stat_recv, parts_send, parts_recv,
    down_send, entry_send, cross_send, block_recv, tile_send, tile_recv, spare_send, spare_recv,
):
    half = count // 2
    depth = half // 2
    lines = count // 2
    middle = half // 2
    rows, cols = slots.shape[1], slots.shape[2]
    lanes = cols // 8
    width = gram_ref.shape[1]
    piece = rows // CHUNKS
    me = lax.axis_index("smp")
    core = lax.axis_index("par")
    line, bit = lax.div(me, 2), lax.rem(me, 2)
    mate = 1 - 2 * bit

    def at(steps):
        return lax.rem(me + steps + count, count)

    load = pltpu.make_async_copy(x_hbm, slots.at[0], load_sem)
    load.start()
    c_load = pltpu.make_async_copy(c_hbm, c_ref, c_sem)
    c_load.start()
    barrier = pltpu.get_barrier_semaphore()
    pl.semaphore_signal(barrier, inc=1, device_id={"par": 1 - core})
    pl.semaphore_signal(barrier, inc=1, device_id={"smp": at(mate)})
    pl.semaphore_signal(barrier, inc=1, device_id={"smp": at(mate), "par": 1 - core})

    @pl.when(line > 0)
    def _():
        pl.semaphore_signal(barrier, inc=1, device_id={"smp": at(-2)})

    @pl.when(line < lines - 1)
    def _():
        pl.semaphore_signal(barrier, inc=1, device_id={"smp": at(2)})

    def pack(value):
        return jnp.concatenate([value[:, lanes * j : lanes * (j + 1)] for j in range(8)], axis=0)

    def unpack(value):
        return jnp.concatenate([value[j : j + 1, :] for j in range(8)], axis=1)

    load.wait()
    pairs[bit] = pack(jnp.sum(slots[0].astype(jnp.float32), axis=0, keepdims=True))
    c_load.wait()
    pl.semaphore_wait(barrier, 3 + jnp.where(line > 0, 1, 0) + jnp.where(line < lines - 1, 1, 0))

    def pair_copy(source):
        return pltpu.make_async_remote_copy(
            src_ref=pairs.at[source], dst_ref=pairs.at[source],
            send_sem=pair_send, recv_sem=pair_recv, device_id={"smp": at(mate)},
        )

    def line_copy(slot, steps):
        return pltpu.make_async_remote_copy(
            src_ref=stats.at[slot], dst_ref=stats.at[slot],
            send_sem=stat_send.at[steps], recv_sem=stat_recv.at[slot],
            device_id={"smp": at(2 * steps)},
        )

    def parts_copy(slot, steps):
        return pltpu.make_async_remote_copy(
            src_ref=parts.at[slot], dst_ref=parts.at[slot],
            send_sem=parts_send.at[steps], recv_sem=parts_recv.at[slot],
            device_id={"smp": at(steps)},
        )

    def block_copy(source, target, chunk, send, device):
        span = pl.ds(pl.multiple_of(chunk * piece, 16), piece)
        return pltpu.make_async_remote_copy(
            src_ref=slots.at[source, span], dst_ref=slots.at[target, span],
            send_sem=send, recv_sem=block_recv.at[target, chunk],
            device_id={"smp": device},
        )

    def down(d, chunk):
        return block_copy(d, d + 1, chunk, down_send.at[d, chunk], at(-2))

    def up(d, chunk):
        return block_copy(d, d - 1, chunk, down_send.at[d, chunk], at(2))

    def entry(chunk):
        return block_copy(0, depth, chunk, entry_send.at[chunk], at(-2 * depth))

    def cross(chunk):
        return block_copy(0, depth + 1, chunk, cross_send.at[chunk], at(mate))

    pair_copy(bit).start()

    @pl.when(line > 0)
    def _():
        for chunk in range(FIRST):
            down(0, chunk).start()

    def tell(q):
        @pl.when(line + q < lines)
        def _():
            if q > 1:
                pl.semaphore_wait(above.at[q - 1], 1)

            @pl.when(line > 0)
            def _():
                pl.semaphore_signal(above.at[q], inc=1, device_id={"smp": at(-2)})

        @pl.when(line - q >= 0)
        def _():
            if q > 1:
                pl.semaphore_wait(below.at[q - 1], 1)

            @pl.when(line < lines - 1)
            def _():
                pl.semaphore_signal(below.at[q], inc=1, device_id={"smp": at(2)})

    for q in range(1, depth + 1):
        tell(q)

    @pl.when(line < depth)
    def _():
        for chunk in range(FIRST):
            entry(chunk).start()

    for q in range(depth + 1, lines):
        tell(q)

    pair_copy(1 - bit).wait_recv()
    stats[line] = pairs[0] + pairs[1]
    each(1, lines, lambda j: line_copy(line, j).start())
    for chunk in range(FIRST, CHUNKS):
        @pl.when(line > 0)
        def _():
            down(0, chunk).start()

        @pl.when(line < depth)
        def _():
            entry(chunk).start()

    for chunk in range(CHUNKS):
        cross(chunk).start()

    def line_at(steps):
        return lax.rem(line + steps, lines)

    def mean_row():
        return unpack(jnp.sum(stats[...], axis=0)) / (rows * count)

    def tile_copy(k, source, low, size):
        span = pl.ds(pl.multiple_of(low, 16), size)
        return pltpu.make_async_remote_copy(
            src_ref=band.at[source, span], dst_ref=band.at[source, span],
            send_sem=tile_send.at[k], recv_sem=tile_recv.at[k],
            device_id={"par": 1 - core},
        )

    def tile_whole(k, source):
        return tile_copy(k, source, k * rows, rows)

    def tile_split(side, source):
        return tile_copy(middle, source, middle * rows + side * (rows // 2), rows // 2)

    def spare_copy(d, tile, source):
        return pltpu.make_async_remote_copy(
            src_ref=spare.at[d],
            dst_ref=band.at[source, pl.ds(pl.multiple_of(tile * rows, 16), rows)],
            send_sem=spare_send.at[d], recv_sem=spare_recv.at[tile, source],
            device_id={"smp": at(mate), "par": jnp.where(tile > middle, 1, 0)},
        )

    def for_mate(d):
        return jnp.logical_or(jnp.logical_and(bit == 0, d > 0), jnp.logical_and(bit == 1, d < depth))

    def centre(d, mean):
        return (slots[d].astype(jnp.float32) - mean).astype(jnp.bfloat16)

    def tile_of(value, which):
        return lax.dot_general(
            value, cent[which], (((1,), (1,)), ((), ())), preferred_element_type=jnp.float32
        )

    def process(d, mean):
        k = 2 * d
        value = centre(d, mean)

        @pl.when(for_mate(d))
        def _():
            spare[d] = tile_of(value, 1)
            spare_copy(d, k - mate, core).start()

        span = pl.ds(pl.multiple_of(k * rows, 16), rows)
        band[core, span] = tile_of(value, 0)

        @pl.when(jnp.logical_or(jnp.logical_and(k > middle, core == 0), jnp.logical_and(k < middle, core == 1)))
        def _():
            tile_whole(k, core).start()

        @pl.when(k == middle)
        def _():
            tile_split(1 - core, core).start()

    def middle_work():
        each(1, lines, lambda j: line_copy(line_at(j), j).wait_recv())
        mean = mean_row()
        cent[0] = centre(0, mean)
        c = c_ref[...]
        c1 = c.astype(jnp.bfloat16).astype(jnp.float32)
        c2 = (c - c1).astype(jnp.bfloat16).astype(jnp.float32)
        c3 = c - c1 - c2
        row = lax.broadcasted_iota(jnp.int32, (16, rows), 0)
        weights = jnp.where(row == 0, c1, jnp.where(row == 1, c2, jnp.where(row == 2, c3, 0.0)))
        sums = jnp.dot(weights.astype(jnp.bfloat16), cent[0], preferred_element_type=jnp.float32)
        parts[me] = pack(sums[0:1] + sums[1:2] + sums[2:3])
        each(1, count, lambda j: parts_copy(me, j).start())
        for chunk in range(CHUNKS):
            cross(chunk).wait_recv()
        cent[1] = centre(depth + 1, mean)
        process(0, mean)

    wraps = line + depth >= lines

    def arrival(step):
        d = jnp.where(wraps, depth - lax.rem(step, depth), 1 + lax.div(step, CHUNKS))
        chunk = jnp.where(wraps, lax.div(step, depth), lax.rem(step, CHUNKS))
        block_copy(d, d, chunk, down_send.at[d, chunk], at(2)).wait_recv()
        inside = line + d < lines

        @pl.when(jnp.logical_and(inside, jnp.logical_and(d < depth, line > 0)))
        def _():
            down(d, chunk).start()

        @pl.when(jnp.logical_and(jnp.logical_not(inside), jnp.logical_and(d > 1, line < lines - 1)))
        def _():
            up(d, chunk).start()

    each(0, MEAN_AFTER, lambda step: arrival(jnp.int32(step)))
    middle_work()
    each(MEAN_AFTER, depth * CHUNKS, lambda step: arrival(jnp.int32(step)))
    mean = mean_row()

    each(1, depth + 1, lambda d: process(d, mean))

    for chunk in range(CHUNKS):
        @pl.when(line > 0)
        def _():
            down(0, chunk).wait_send()

        @pl.when(line < depth)
        def _():
            entry(chunk).wait_send()

        cross(chunk).wait_send()

    def leave(d):
        inside = line + d < lines
        for chunk in range(CHUNKS):
            @pl.when(jnp.logical_and(inside, jnp.logical_and(d < depth, line > 0)))
            def _():
                down(d, chunk).wait_send()

            @pl.when(jnp.logical_and(jnp.logical_not(inside), jnp.logical_and(d > 1, line < lines - 1)))
            def _():
                up(d, chunk).wait_send()

    each(1, depth + 1, leave)
    pair_copy(bit).wait_send()
    each(1, lines, lambda j: line_copy(line, j).wait_send())
    each(1, count, lambda j: parts_copy(me, j).wait_send())
    each(1, count, lambda j: parts_copy(at(j), j).wait_recv())
    update_ref[...] = unpack(jnp.sum(parts[...], axis=0))

    def swapped(d):
        k = 2 * d

        @pl.when(for_mate(d))
        def _():
            spare_copy(d, k - mate, core).wait_send()

        @pl.when(jnp.logical_or(jnp.logical_and(k > middle, core == 0), jnp.logical_and(k < middle, core == 1)))
        def _():
            tile_whole(k, core).wait_send()

        @pl.when(jnp.logical_or(jnp.logical_and(k > middle, core == 1), jnp.logical_and(k < middle, core == 0)))
        def _():
            tile_whole(k, 1 - core).wait_recv()

        @pl.when(k == middle)
        def _():
            tile_split(1 - core, core).wait_send()
            tile_split(core, 1 - core).wait_recv()

        @pl.when(jnp.logical_and(d > 0, core == jnp.where(k - 1 > middle, 1, 0)))
        def _():
            for source in range(2):
                spare_copy(d, k - 1, source).wait_recv()

    each(0, depth + 1, swapped)
    mine = pl.ds(pl.multiple_of(core * width, 16), width)
    gram_ref[...] = (band[0, mine] + band[1, mine]).T


def on_device(log_derivs, coeffs):
    rows, cols = log_derivs.shape
    count = lax.axis_size("smp")
    half = count // 2
    depth = half // 2
    lines = count // 2
    band = (half + 1) * rows
    width = band // lax.axis_size("par")
    block = rows * cols * 2
    dma = pltpu.SemaphoreType.DMA
    gram, update = pl.pallas_call(
        functools.partial(kernel, count),
        out_shape=(
            jax.ShapeDtypeStruct((rows, width), jnp.float32),
            jax.ShapeDtypeStruct((1, cols), jnp.float32),
        ),
        in_specs=[pl.BlockSpec(memory_space=pltpu.HBM)] * 2,
        out_specs=(pl.BlockSpec(memory_space=pltpu.VMEM), pl.BlockSpec(memory_space=pltpu.VMEM)),
        scratch_shapes=[
            pltpu.VMEM((depth + 2, rows, cols), jnp.bfloat16),
            pltpu.VMEM((2, rows, cols), jnp.bfloat16),
            pltpu.VMEM((1, rows), jnp.float32),
            pltpu.VMEM((2, 8, cols // 8), jnp.float32),
            pltpu.VMEM((lines, 8, cols // 8), jnp.float32),
            pltpu.VMEM((count, 8, cols // 8), jnp.float32),
            pltpu.VMEM((2, band, rows), jnp.float32),
            pltpu.VMEM((depth + 1, rows, rows), jnp.float32),
            dma, dma,
            pltpu.SemaphoreType.REGULAR((lines,)), pltpu.SemaphoreType.REGULAR((lines,)),
            dma, dma, dma((lines,)), dma((lines,)), dma((count,)), dma((count,)),
            dma((depth + 1, CHUNKS)), dma((CHUNKS,)), dma((CHUNKS,)),
            dma((depth + 2, CHUNKS)), dma((half + 1,)), dma((half + 1,)),
            dma((depth + 1,)), dma((half + 1, 2)),
        ],
        compiler_params=pltpu.CompilerParams(
            collective_id=0,
            has_side_effects=True,
            vmem_limit_bytes=48 * 2**20 if half > 16 else 16 * 2**20,
        ),
        cost_estimate=pl.CostEstimate(
            flops=4 * rows * cols * width, bytes_accessed=2 * block, transcendentals=0
        ),
    )(log_derivs, coeffs.reshape(1, rows))
    return gram, update.reshape(cols)


def solution(mesh):
    return jax.shard_map(
        on_device,
        mesh=mesh,
        in_specs=(P(("grp", "smp"), "par"), P(("grp", "smp"))),
        out_specs=(P(("grp", "smp"), "par"), P(("grp", "par"))),
        check_vma=False,
    )
```

time: 27.7 us -> 24.9 us (0.90)
  Pallas kernels: 24.1 us -> 21.3 us
    pallas_call x1, Pallas kernels: 24.1 us -> 21.3 us  [on_device(): pl.pallas_call(functools.partial(kernel, count), out_shape=(jax.ShapeDtyp...]
where the time goes in v3:
time: 24.9 us; the launch traced here: 24.7 us
  Pallas kernels  21.3 us (86%)
  local copies, waits for them, and re-layouts  2.81 us (11%)
  between operations  0.65 us (3%)
    pallas_call x1, Pallas kernels, on_device(): pl.pallas_call(functools.partial(kernel, count), out_shape=(jax.ShapeDtyp...  21.3 us
    unnamed x6, local copies, waits for them, and re-layouts  2.81 us

profile of v3, /device:TPU:31, one launch (start us, length us, event | category | flops | bytes accessed | tf_op | source)
XLA Modules:
  0.0 24.7 jit_solution(5735026276749103103)
XLA Ops:
  0.6 0.0 copy-start.1
  0.6 0.6 %copy-done.1 = f32[96]{0:T(128)S(1)} copy-done((f32[96]{0:T(128)S(1)}, f32[96]{0:T(128)}, u32[]{:S(2)}) %copy-start.1) | copy-done | bytes 408
  1.3 0.0 copy-start
  1.3 0.9 %copy-done = bf16[96,1024]{1,0:T(8,128)(2,1)S(1)} copy-done((bf16[96,1024]{1,0:T(8,128)(2,1)S(1)}, bf16[96,1024]{1,0:T(8,128)(2,1)}, u32[]{:S(2)}) %copy-start) | copy-done | bytes 196632
  2.2 21.3 %shard_map.41 = (f32[96,240]{1,0:T(8,128)S(1)}, f32[1,1024]{1,0:T(1,128)S(1)}) custom-call(bf16[96,1024]{1,0:T(8,128)(2,1)S(1)} %copy-done, f32[1,96]{1,0:T(1,128)S(1)} %bitcast.3), custom_call_target="tpu_custom_call" | custom-call | flops 94371840 | bytes 393216 | tf_op jit(solution)/shard_map/pallas_call | solution.py:335
  23.5 0.6 %copy.6 = f32[96,240]{1,0:T(8,128)} copy(f32[96,240]{1,0:T(8,128)S(1)} %get-tuple-element.8) | data formatting | bytes 184320
  24.1 0.6 %copy.7 = f32[1024]{0:T(1024)} copy(f32[1024]{0:T(1024)S(1)} %bitcast.2) | data formatting | bytes 8192
Async XLA Ops:
  0.6 0.7 %copy-start.1 = (f32[96]{0:T(128)S(1)}, f32[96]{0:T(128)}, u32[]{:S(2)}) copy-start(f32[96]{0:T(128)} %param.3) | copy-start | bytes 1156
  1.3 0.9 %copy-start = (bf16[96,1024]{1,0:T(8,128)(2,1)S(1)}, bf16[96,1024]{1,0:T(8,128)(2,1)}, u32[]{:S(2)}) copy-start(bf16[96,1024]{1,0:T(8,128)(2,1)} %x_hbm.1) | copy-start | bytes 589828
